TPU v7x, 32 devices: a whole 2x2x4 slice. The times are simulated.
32 devices in a mesh: tm: 8 (over y, x, core), space: 4 (over z).
Axes of the slice: x: 2, y: 2, z: 4, core: 2. Of those that a mesh axis runs over, the one named last changes fastest.
Arguments:
- queries: bfloat16 [8, 1024, 512], P('tm', 'space'), may hold values from -8 to 8
- key_tokens: bfloat16 [8, 1024, 512], P('tm', 'space'), may hold values from -8 to 8
- values: bfloat16 [8, 1024, 512], P('tm', 'space'), may hold values from -8 to 8
- near_list: int32 [8, 4, 8], replicated, may hold values from 0 to 11, as said below
- near_count: int32 [8, 4], replicated, may hold values from 1 to 8, as said below
- dist_band: int32 [8], replicated, may hold values from 0 to 3, as said below
- band_factor: int32 [3], replicated, may hold values from 1 to 4, as said below
Outputs:
- attended: bfloat16 [8, 1024, 512], P('tm', 'space')
Inputs may be any that keep to these rules, and one draw needn't show every extreme that they name: `near_list`: each entry is distinct within its list, never names a frame outside 0 to 7, and the first entry of block b is block b of the same frame. `near_count`: some query block of some frame lists 8 live blocks. `dist_band`: nondecreasing in the distance; 0 exactly for distances 0 and 1, 3 at distance 8 - 1. `band_factor`: each entry is 1, 2 or 4, and some entry is 4.
All inputs are finite; a program needn't handle non-finite values.
Results may differ from a plain program's by a relative error of at most 0.0028.
The roundings to bfloat16 on the way count: a program that leaves them out, or rounds other values in their place, can miss the bound.
Values may be sent and summed in bfloat16 or wider, within the bound.
A program may use at most 64 MiB of HBM per device.

v0:
```python
import math
import jax
import jax.numpy as jnp
from jax import lax
from jax.sharding import PartitionSpec as P

HD = 128
POOL = 128
lowest_score = -1e30


def extended(block, sides, width):
    for axis, dim in sides:
        count = lax.axis_size(axis)
        forward = [(i, i + 1) for i in range(count - 1)]
        backward = [(target, source) for source, target in forward]
        low = lax.ppermute(
            lax.slice_in_dim(block, block.shape[dim] - width, None, axis=dim), axis, forward
        )
        high = lax.ppermute(lax.slice_in_dim(block, 0, width, axis=dim), axis, backward)
        block = jnp.concatenate([low, block, high], axis=dim)
    return block


def lookup(table_values, positions):
    slot_ids = jnp.arange(table_values.shape[0], dtype=jnp.int32)
    picked = jnp.where(positions[:, None] == slot_ids[None, :], table_values[None, :], 0)
    return jnp.sum(picked, axis=1)


def coarsen(pooled, factor):
    frame_count, far_rows, head_count, head_size = pooled.shape
    widened = pooled.astype(jnp.float32)
    pair_means = jnp.mean(
        widened.reshape(frame_count, far_rows // 2, 2, head_count, head_size), axis=2
    ).astype(jnp.bfloat16)
    quad_means = jnp.mean(
        widened.reshape(frame_count, far_rows // 4, 4, head_count, head_size), axis=2
    ).astype(jnp.bfloat16)
    pair_means = jnp.repeat(pair_means, 2, axis=1)
    quad_means = jnp.repeat(quad_means, 4, axis=1)
    choose_factor = factor[:, None, None, None]
    return jnp.where(
        choose_factor == 1, pooled, jnp.where(choose_factor == 2, pair_means, quad_means)
    )


def attend_block(query_rows, near_k, near_v, near_ok, far_k, far_v, far_bias, far_ok):
    score_scale = 1.0 / math.sqrt(query_rows.shape[-1])
    near_scores = (
        jnp.einsum("bhd,khd->hbk", query_rows, near_k, preferred_element_type=jnp.float32)
        * score_scale
    )
    far_scores = (
        jnp.einsum("bhd,khd->hbk", query_rows, far_k, preferred_element_type=jnp.float32)
        * score_scale
        + far_bias[None, None, :]
    )
    near_scores = jnp.where(near_ok[None, None, :], near_scores, lowest_score)
    far_scores = jnp.where(far_ok[None, None, :], far_scores, lowest_score)
    row_top = jnp.maximum(
        jnp.max(near_scores, axis=-1, keepdims=True), jnp.max(far_scores, axis=-1, keepdims=True)
    )
    near_weights = jnp.where(near_ok[None, None, :], jnp.exp(near_scores - row_top), 0.0)
    far_weights = jnp.where(far_ok[None, None, :], jnp.exp(far_scores - row_top), 0.0)
    denominator = jnp.sum(near_weights, axis=-1) + jnp.sum(far_weights, axis=-1)
    weighted = jnp.einsum(
        "hbk,khd->bhd",
        near_weights.astype(jnp.bfloat16),
        near_v,
        preferred_element_type=jnp.float32,
    )
    weighted = weighted + jnp.einsum(
        "hbk,khd->bhd", far_weights.astype(jnp.bfloat16), far_v, preferred_element_type=jnp.float32
    )
    return (weighted / jnp.transpose(denominator)[:, :, None]).astype(jnp.bfloat16)


def attend_frame(
    query_frame,
    key_rim,
    value_rim,
    pooled_k,
    pooled_v,
    lists,
    counts,
    dist_band,
    band_factor,
    frame_index,
):
    frame_tokens, head_count, head_size = query_frame.shape
    block_count, list_length = lists.shape
    block_rows = frame_tokens // block_count
    frame_count, far_rows = (pooled_k.shape[0], pooled_k.shape[1])
    distance = jnp.abs(jnp.arange(frame_count, dtype=jnp.int32) - frame_index)
    band_index = lookup(dist_band, distance)
    factor = jnp.maximum(lookup(band_factor, band_index - 1), 1)
    far_k = coarsen(pooled_k, factor).reshape(frame_count * far_rows, head_count, head_size)
    far_v = coarsen(pooled_v, factor).reshape(frame_count * far_rows, head_count, head_size)
    far_bias = jnp.repeat(-jnp.log(factor.astype(jnp.float32)), far_rows)
    far_ok = jnp.repeat(distance >= 2, far_rows)
    key_blocks = key_rim.reshape(3 * block_count, block_rows, head_count, head_size)
    value_blocks = value_rim.reshape(3 * block_count, block_rows, head_count, head_size)

    def one_block(block_index):
        block_ids = lax.dynamic_index_in_dim(lists, block_index, 0, keepdims=False)
        live_slots = lax.dynamic_index_in_dim(counts, block_index, 0, keepdims=False)
        near_k = jnp.take(key_blocks, block_ids, axis=0).reshape(
            list_length * block_rows, head_count, head_size
        )
        near_v = jnp.take(value_blocks, block_ids, axis=0).reshape(
            list_length * block_rows, head_count, head_size
        )
        near_ok = jnp.repeat(jnp.arange(list_length, dtype=jnp.int32) < live_slots, block_rows)
        query_rows = lax.dynamic_slice_in_dim(query_frame, block_index * block_rows, block_rows, 0)
        return attend_block(query_rows, near_k, near_v, near_ok, far_k, far_v, far_bias, far_ok)

    results = lax.map(one_block, jnp.arange(block_count, dtype=jnp.int32))
    return results.reshape(frame_tokens, head_count, head_size)


def local(queries, key_tokens, values, near_list, near_count, dist_band, band_factor):
    tokens_dev = queries.shape[1]
    features = queries.shape[2]
    head_count = features // HD
    frame_index = lax.axis_index("tm")
    split_shape = (1, tokens_dev, head_count, HD)
    split_q, split_k, split_v = (
        lax.all_to_all(
            queries.reshape(split_shape), "space", split_axis=2, concat_axis=1, tiled=True
        ),
        lax.all_to_all(
            key_tokens.reshape(split_shape), "space", split_axis=2, concat_axis=1, tiled=True
        ),
        lax.all_to_all(
            values.reshape(split_shape), "space", split_axis=2, concat_axis=1, tiled=True
        ),
    )
    head_pair = jnp.stack([split_k, split_v], axis=1)
    rim_heads = extended(head_pair, (("tm", 0),), 1)
    key_rim = rim_heads[:, 0]
    value_rim = rim_heads[:, 1]
    frame_tokens = key_rim.shape[1]
    local_heads = key_rim.shape[2]
    own_pair = jnp.stack([key_rim[1], value_rim[1]], axis=0)
    pooled_heads = jnp.mean(
        own_pair.reshape(2, frame_tokens // POOL, POOL, local_heads, HD), axis=2, dtype=jnp.float32
    ).astype(jnp.bfloat16)
    far_pair = lax.all_gather(pooled_heads[None], "tm", axis=0, tiled=True)
    lists = lax.dynamic_index_in_dim(near_list, frame_index, 0, keepdims=False)
    counts = lax.dynamic_index_in_dim(near_count, frame_index, 0, keepdims=False)
    frame_output = attend_frame(
        split_q[0],
        key_rim,
        value_rim,
        far_pair[:, 0],
        far_pair[:, 1],
        lists,
        counts,
        dist_band,
        band_factor,
        frame_index,
    )
    returned = lax.all_to_all(frame_output[None], "space", split_axis=1, concat_axis=2, tiled=True)
    return returned.reshape(1, tokens_dev, features)


def solution(mesh):
    return jax.shard_map(
        local,
        mesh=mesh,
        in_specs=(
            P("tm", "space", None),
            P("tm", "space", None),
            P("tm", "space", None),
            P(),
            P(),
            P(),
            P(),
        ),
        out_specs=P("tm", "space", None),
        check_vma=False,
    )
```

profile of v0, /device:TPU:0, one launch (start us, length us, event | category | flops | bytes accessed | tf_op | source)
XLA Modules:
  0.0 123.3 jit_solution(3960450113721223402)
XLA Ops:
  0.0 1.8 %copy.51 = bf16[1,256,512]{1,2,0:T(8,128)(2,1)} copy(bf16[1,256,512]{2,1,0:T(8,128)(2,1)} %param.12) | data formatting | bytes 524288 | tf_op args[1]
  1.8 6.3 %all-to-all-start = ((bf16[1,256,4,128]{1,3,0,2:T(8,128)(2,1)}), bf16[1,256,4,128]{1,3,0,2:T(8,128)(2,1)S(1)}, u32[]{:S(2)}, u32[]{:S(2)}) async-start(bf16[1,256,4,128]{1,3,0,2:T(8,128)(2,1)} %bitcast.2), calls=%async_computation | async-start | bytes 524288 | tf_op jit(solution)/shard_map/all_to_all | solution.py:132
  10.1 1.8 %copy.54 = bf16[1,256,512]{1,2,0:T(8,128)(2,1)} copy(bf16[1,256,512]{2,1,0:T(8,128)(2,1)} %param.13) | data formatting | bytes 524288 | tf_op args[2]
  11.9 1.8 %copy.57 = bf16[1,256,512]{1,2,0:T(8,128)(2,1)} copy(bf16[1,256,512]{2,1,0:T(8,128)(2,1)} %param.11) | data formatting | bytes 524288 | tf_op args[0]
  13.8 3.2 %all-to-all-done = bf16[1,256,4,128]{1,3,0,2:T(8,128)(2,1)S(1)} async-done(((bf16[1,256,4,128]{1,3,0,2:T(8,128)(2,1)}), bf16[1,256,4,128]{1,3,0,2:T(8,128)(2,1)S(1)}, u32[]{:S(2)}, u32[]{:S(2)}) %all-to-all-start) | async-done | bytes 262176 | tf_op jit(solution)/shard_map/all_to_all | solution.py:132
  17.0 3.4 %all-to-all-start.1 = ((bf16[1,256,4,128]{1,3,0,2:T(8,128)(2,1)}), bf16[1,256,4,128]{1,3,0,2:T(8,128)(2,1)S(1)}, u32[]{:S(2)}, u32[]{:S(2)}) async-start(bf16[1,256,4,128]{1,3,0,2:T(8,128)(2,1)} %bitcast.7), calls=%async_computation.1 | async-start | bytes 524288 | tf_op jit(solution)/shard_map/all_to_all | solution.py:135
  20.7 6.8 %all-to-all-done.1 = bf16[1,256,4,128]{1,3,0,2:T(8,128)(2,1)S(1)} async-done(((bf16[1,256,4,128]{1,3,0,2:T(8,128)(2,1)}), bf16[1,256,4,128]{1,3,0,2:T(8,128)(2,1)S(1)}, u32[]{:S(2)}, u32[]{:S(2)}) %all-to-all-start.1) | async-done | bytes 262176 | tf_op jit(solution)/shard_map/all_to_all | solution.py:135
  27.5 3.4 %all-to-all-start.2 = ((bf16[1,256,4,128]{1,3,0,2:T(8,128)(2,1)}), bf16[1,256,4,128]{1,3,0,2:T(8,128)(2,1)S(1)}, u32[]{:S(2)}, u32[]{:S(2)}) async-start(bf16[1,256,4,128]{1,3,0,2:T(8,128)(2,1)} %bitcast.13), calls=%async_computation.2 | async-start | bytes 524288 | tf_op jit(solution)/shard_map/all_to_all | solution.py:129
  31.1 1.3 %collective-permute-start = (bf16[1,2,1024,1,128]{4,2,3,1,0:T(8,128)(2,1)S(1)}, bf16[1,2,1024,1,128]{4,2,3,1,0:T(8,128)(2,1)S(1)}, u32[]{:S(2)}, u32[]{:S(2)}) collective-permute-start(bf16[1,2,1024,1,128]{4,2,3,1,0:T(8,128)(2,1)S(1)} %pad_maximum_fusion.1), channel_id=1, source_target_pairs={{0,4},{4,8},{8,12},{12,16},{16,20},{20,24},{24,28},{1,5},{5,9},{9,... | collective-permute-start | bytes 1572872 | tf_op jit(solution)/shard_map/ppermute | solution.py:17
  32.4 1.3 %collective-permute-start.1 = (bf16[1,2,1024,1,128]{4,2,3,1,0:T(8,128)(2,1)S(1)}, bf16[1,2,1024,1,128]{4,2,3,1,0:T(8,128)(2,1)S(1)}, u32[]{:S(2)}, u32[]{:S(2)}) collective-permute-start(bf16[1,2,1024,1,128]{4,2,3,1,0:T(8,128)(2,1)S(1)} %pad_maximum_fusion.1), channel_id=1, source_target_pairs={{4,0},{8,4},{12,8},{16,12},{20,16},{24,20},{28,24},{5,1},{9,5},{13... | collective-permute-start | bytes 1572872 | tf_op jit(solution)/shard_map/ppermute | solution.py:20
  33.8 15.5 %all-gather = bf16[16,8,128]{2,1,0:T(8,128)(2,1)S(1)} all-gather(bf16[2,8,128]{2,1,0:T(8,128)(2,1)S(1)} %multiply_convert_fusion.4), channel_id=2, replica_groups=mesh['tm'=8,'space'=4] {'tm'}, dimensions={0}, use_global_device_ids=true | all-gather | bytes 36864 | tf_op jit(solution)/shard_map/all_gather | solution.py:149
  51.7 51.8 %while.11 = (s32[]{:T(128)}, bf16[4,256,1,128]{3,1,0,2:T(8,128)(2,1)}, s32[4]{0:T(128)S(1)}, s32[4,8]{1,0:T(4,128)S(1)}, bf16[12,256,1,128]{3,1,0,2:T(8,128)(2,1...) while((s32[]{:T(128)}, ...), condition=%wide.region_12.14_spmd.clone, body=%wide.region_7.13_spmd.clone.sunk | while | flops 282329664 | bytes 14615961 | solution.py:118
  54.3 1.8 %gather_fusion = bf16[8,256,128]{2,1,0:T(8,128)(2,1)S(1)} fusion(bf16[12,256,128]{2,1,0:T(8,128)(2,1)} %bitcast.129, s32[1024]{0:T(1024)S(1)} %pad_clamp_fusion.2), kind=kCustom, calls=%fused_computation.clone.clone.1 | custom fusion | bytes 1048608 | tf_op jit(solution)/shard_map/while/body/eval_jaxpr/jit(_take)/gather | solution.py:111
  59.8 1.4 %fusion.55 = (f32[256]{0:T(256)S(1)}, f32[256,2048]{1,0:T(8,128)S(1)}) fusion(bf16[2048,128]{1,0:T(8,128)(2,1)S(1)} %bitcast.134, bf16[1024,1,128]{2,0,1:T(8,128)(2,1)} %get-tuple-element.267, s32[]{:T(128)S(6)} %select_n.160, pred[2048]{0:T(1024)(128)(4,1)S(1)} %broadcast_in_dim.258), kind=kOutput, calls=%fused_computation.71.clone.1 | convolution fusion | flops 135790336 | bytes 2690052 | tf_op jit(solution)/shard_map/while/body/eval_jaxpr/bhd,khd->hbk/dot_general | solution.py:51
  67.3 1.8 %gather_fusion = bf16[8,256,128]{2,1,0:T(8,128)(2,1)S(1)} fusion(bf16[12,256,128]{2,1,0:T(8,128)(2,1)} %bitcast.129, s32[1024]{0:T(1024)S(1)} %pad_clamp_fusion.2), kind=kCustom, calls=%fused_computation.clone.clone.1 | custom fusion | bytes 1048608 | tf_op jit(solution)/shard_map/while/body/eval_jaxpr/jit(_take)/gather | solution.py:111
  72.7 1.4 %fusion.55 = (f32[256]{0:T(256)S(1)}, f32[256,2048]{1,0:T(8,128)S(1)}) fusion(bf16[2048,128]{1,0:T(8,128)(2,1)S(1)} %bitcast.134, bf16[1024,1,128]{2,0,1:T(8,128)(2,1)} %get-tuple-element.267, s32[]{:T(128)S(6)} %select_n.160, pred[2048]{0:T(1024)(128)(4,1)S(1)} %broadcast_in_dim.258), kind=kOutput, calls=%fused_computation.71.clone.1 | convolution fusion | flops 135790336 | bytes 2690052 | tf_op jit(solution)/shard_map/while/body/eval_jaxpr/bhd,khd->hbk/dot_general | solution.py:51
  80.3 1.8 %gather_fusion = bf16[8,256,128]{2,1,0:T(8,128)(2,1)S(1)} fusion(bf16[12,256,128]{2,1,0:T(8,128)(2,1)} %bitcast.129, s32[1024]{0:T(1024)S(1)} %pad_clamp_fusion.2), kind=kCustom, calls=%fused_computation.clone.clone.1 | custom fusion | bytes 1048608 | tf_op jit(solution)/shard_map/while/body/eval_jaxpr/jit(_take)/gather | solution.py:111
  85.7 1.4 %fusion.55 = (f32[256]{0:T(256)S(1)}, f32[256,2048]{1,0:T(8,128)S(1)}) fusion(bf16[2048,128]{1,0:T(8,128)(2,1)S(1)} %bitcast.134, bf16[1024,1,128]{2,0,1:T(8,128)(2,1)} %get-tuple-element.267, s32[]{:T(128)S(6)} %select_n.160, pred[2048]{0:T(1024)(128)(4,1)S(1)} %broadcast_in_dim.258), kind=kOutput, calls=%fused_computation.71.clone.1 | convolution fusion | flops 135790336 | bytes 2690052 | tf_op jit(solution)/shard_map/while/body/eval_jaxpr/bhd,khd->hbk/dot_general | solution.py:51
  93.2 1.8 %gather_fusion = bf16[8,256,128]{2,1,0:T(8,128)(2,1)S(1)} fusion(bf16[12,256,128]{2,1,0:T(8,128)(2,1)} %bitcast.129, s32[1024]{0:T(1024)S(1)} %pad_clamp_fusion.2), kind=kCustom, calls=%fused_computation.clone.clone.1 | custom fusion | bytes 1048608 | tf_op jit(solution)/shard_map/while/body/eval_jaxpr/jit(_take)/gather | solution.py:111
  98.7 1.4 %fusion.55 = (f32[256]{0:T(256)S(1)}, f32[256,2048]{1,0:T(8,128)S(1)}) fusion(bf16[2048,128]{1,0:T(8,128)(2,1)S(1)} %bitcast.134, bf16[1024,1,128]{2,0,1:T(8,128)(2,1)} %get-tuple-element.267, s32[]{:T(128)S(6)} %select_n.160, pred[2048]{0:T(1024)(128)(4,1)S(1)} %broadcast_in_dim.258), kind=kOutput, calls=%fused_computation.71.clone.1 | convolution fusion | flops 135790336 | bytes 2690052 | tf_op jit(solution)/shard_map/while/body/eval_jaxpr/bhd,khd->hbk/dot_general | solution.py:51
  100.4 1.0 fusion.54
  103.6 1.4 %copy.69 = bf16[1,1024,1,128]{3,2,0,1:T(2,128)(2,1)S(1)} copy(bf16[1,1024,1,128]{3,1,2,0:T(8,128)(2,1)} %bitcast.155) | data formatting | bytes 524288 | tf_op jit(solution)/shard_map/broadcast_in_dim;reshape | solution.py:164
  105.4 2.2 %reduce.19 = bf16[1024,128]{1,0:T(8,128)(2,1)S(1)} reduce(bf16[1024,1,1,128]{3,2,1,0:T(2,128)(2,1)S(1)} %bitcast.145, bf16[]{:T(256)} %broadcast.251), dimensions={1,2}, to_apply=%bitcast.101.reduce_sub_computation | reduce | bytes 524290
  107.7 14.2 %all_to_all.60 = bf16[4,2,16384]{2,1,0:T(2,128)(2,1)S(1)} all-to-all(bf16[4,2,16384]{2,1,0:T(2,128)(2,1)S(1)} %reshape.508), channel_id=1, replica_groups=mesh['tm'=8,'space'=4] {'space'}, dimensions={0} | all-to-all | bytes 524288 | tf_op jit(solution)/shard_map/all_to_all | solution.py:164
  (145 shorter events, 34.5 us)
Async XLA Ops:
  0.0 20.5 %copy-start = (s32[8,4,8]{2,1,0:T(4,128)S(1)}, s32[8,4,8]{2,1,0:T(4,128)}, u32[]{:S(2)}) copy-start(s32[8,4,8]{2,1,0:T(4,128)} %param.14) | copy-start | bytes 3076
  0.0 13.6 %copy-start.2 = (s32[8,4]{0,1:T(4,128)S(1)}, s32[8,4]{0,1:T(4,128)}, u32[]{:S(2)}) copy-start(s32[8,4]{0,1:T(4,128)} %param.15) | copy-start | bytes 388
  1.8 15.2 %all-to-all-start = ((bf16[1,256,4,128]{1,3,0,2:T(8,128)(2,1)}), bf16[1,256,4,128]{1,3,0,2:T(8,128)(2,1)S(1)}, u32[]{:S(2)}, u32[]{:S(2)}) async-start(bf16[1,256,4,128]{1,3,0,2:T(8,128)(2,1)} %bitcast.2), calls=%async_computation | async-start | bytes 524288 | tf_op jit(solution)/shard_map/all_to_all | solution.py:132
  17.0 10.4 %all-to-all-start.1 = ((bf16[1,256,4,128]{1,3,0,2:T(8,128)(2,1)}), bf16[1,256,4,128]{1,3,0,2:T(8,128)(2,1)S(1)}, u32[]{:S(2)}, u32[]{:S(2)}) async-start(bf16[1,256,4,128]{1,3,0,2:T(8,128)(2,1)} %bitcast.7), calls=%async_computation.1 | async-start | bytes 524288 | tf_op jit(solution)/shard_map/all_to_all | solution.py:135
  27.5 22.1 %all-to-all-start.2 = ((bf16[1,256,4,128]{1,3,0,2:T(8,128)(2,1)}), bf16[1,256,4,128]{1,3,0,2:T(8,128)(2,1)S(1)}, u32[]{:S(2)}, u32[]{:S(2)}) async-start(bf16[1,256,4,128]{1,3,0,2:T(8,128)(2,1)} %bitcast.13), calls=%async_computation.2 | async-start | bytes 524288 | tf_op jit(solution)/shard_map/all_to_all | solution.py:129
  31.1 19.4 %collective-permute-start = (bf16[1,2,1024,1,128]{4,2,3,1,0:T(8,128)(2,1)S(1)}, bf16[1,2,1024,1,128]{4,2,3,1,0:T(8,128)(2,1)S(1)}, u32[]{:S(2)}, u32[]{:S(2)}) collective-permute-start(bf16[1,2,1024,1,128]{4,2,3,1,0:T(8,128)(2,1)S(1)} %pad_maximum_fusion.1), channel_id=1, source_target_pairs={{0,4},{4,8},{8,12},{12,16},{16,20},{20,24},{24,28},{1,5},{5,9},{9,... | collective-permute-start | bytes 1572872 | tf_op jit(solution)/shard_map/ppermute | solution.py:17
  32.4 18.1 %collective-permute-start.1 = (bf16[1,2,1024,1,128]{4,2,3,1,0:T(8,128)(2,1)S(1)}, bf16[1,2,1024,1,128]{4,2,3,1,0:T(8,128)(2,1)S(1)}, u32[]{:S(2)}, u32[]{:S(2)}) collective-permute-start(bf16[1,2,1024,1,128]{4,2,3,1,0:T(8,128)(2,1)S(1)} %pad_maximum_fusion.1), channel_id=1, source_target_pairs={{4,0},{8,4},{12,8},{16,12},{20,16},{24,20},{28,24},{5,1},{9,5},{13... | collective-permute-start | bytes 1572872 | tf_op jit(solution)/shard_map/ppermute | solution.py:20
  61.2 2.2 %copy-start.1 = (bf16[8,256,1,128]{3,1,0,2:T(8,128)(2,1)S(1)}, bf16[8,256,1,128]{3,1,0,2:T(8,128)(2,1)}, u32[]{:S(2)}) copy-start(bf16[8,256,1,128]{3,1,0,2:T(8,128)(2,1)} %get-tuple-element.225) | copy-start | bytes 1572868 | tf_op jit(solution)/shard_map/while
  74.1 2.2 %copy-start.1 = (bf16[8,256,1,128]{3,1,0,2:T(8,128)(2,1)S(1)}, bf16[8,256,1,128]{3,1,0,2:T(8,128)(2,1)}, u32[]{:S(2)}) copy-start(bf16[8,256,1,128]{3,1,0,2:T(8,128)(2,1)} %get-tuple-element.225) | copy-start | bytes 1572868 | tf_op jit(solution)/shard_map/while
  87.1 2.2 %copy-start.1 = (bf16[8,256,1,128]{3,1,0,2:T(8,128)(2,1)S(1)}, bf16[8,256,1,128]{3,1,0,2:T(8,128)(2,1)}, u32[]{:S(2)}) copy-start(bf16[8,256,1,128]{3,1,0,2:T(8,128)(2,1)} %get-tuple-element.225) | copy-start | bytes 1572868 | tf_op jit(solution)/shard_map/while
  100.0 2.2 %copy-start.1 = (bf16[8,256,1,128]{3,1,0,2:T(8,128)(2,1)S(1)}, bf16[8,256,1,128]{3,1,0,2:T(8,128)(2,1)}, u32[]{:S(2)}) copy-start(bf16[8,256,1,128]{3,1,0,2:T(8,128)(2,1)} %get-tuple-element.225) | copy-start | bytes 1572868 | tf_op jit(solution)/shard_map/while
where the time goes:
time: 124 us; the launch traced here: 123 us
  local copies, waits for them, and re-layouts  30.9 us (25%)
  blocking collectives  29.7 us (24%)
  starting transfers between devices  15.7 us (13%)
  other arithmetic  13.3 us (11%)
  matrix products  12.8 us (10%)
  loops' own time  10.6 us (9%)
  waiting for transfers between devices  9.98 us (8%)
    all_gather x1, blocking collectives, local(): far_pair = lax.all_gather(pooled_heads[None], 'tm', axis=0, tiled=True)  15.5 us
    all_to_all x1, blocking collectives, local(): lax.all_to_all(frame_output[None], 'space', split_axis=1, concat_axis=2,...  14.2 us
    another operation x1, loops' own time, attend_frame(): results = lax.map(one_block, jnp.arange(block_count, dtype=jnp.int32))  10.6 us
    gather x4, local copies, waits for them, and re-layouts, one_block(): jnp.take(value_blocks, block_ids, axis=0)  7.12 us
    all_to_all x1, waiting for transfers between devices, local(): lax.all_to_all(values.reshape(split_shape), 'space', split_axis=2, concat...  6.76 us
    all_to_all x1, starting transfers between devices, local(): lax.all_to_all(key_tokens.reshape(split_shape), 'space', split_axis=2, co...  6.32 us
    unnamed x11, local copies, waits for them, and re-layouts  6.28 us
    dot_general x4, matrix products, attend_block(): jnp.einsum('bhd,khd->hbk', query_rows, near_k, preferred_element_type=jnp...  5.48 us
  transfers between devices with their start and end apart: 5, of which 2 were waited for; matrix products, arithmetic and copies ran while one was open for 6% of the time, Pallas kernels for 0%

commit v1 on v0

--- a/solution.py
+++ b/solution.py
@@ -161,7 +161,20 @@
         band_factor,
         frame_index,
     )
-    returned = lax.all_to_all(frame_output[None], "space", split_axis=1, concat_axis=2, tiled=True)
+    ways, here = (lax.axis_size("space"), lax.axis_index("space"))
+    width_2 = frame_output[None].shape[1] // ways
+    lengths = list(frame_output[None].shape)
+    lengths[1] = width_2
+    height = lengths[2]
+    lengths[2] = height * ways
+    returned = jnp.zeros(lengths, frame_output[None].dtype)
+    for mask in range(ways):
+        part = lax.dynamic_slice_in_dim(
+            frame_output[None], (here ^ mask) * width_2, width_2, axis=1
+        )
+        if mask:
+            part = lax.ppermute(part, "space", [(d, d ^ mask) for d in range(ways)])
+        returned = lax.dynamic_update_slice_in_dim(returned, part, (here ^ mask) * height, axis=2)
     return returned.reshape(1, tokens_dev, features)
 
 

time: 124 us -> 120 us (0.968)
  blocking collectives: 29.7 us -> 15.5 us
  waiting for transfers between devices: 9.98 us -> 15.8 us
  starting transfers between devices: 15.7 us -> 20.3 us
  other arithmetic: 13.3 us -> 11.1 us
  local copies, waits for them, and re-layouts: 30.9 us -> 32.7 us
    all_to_all x1 -> x0, blocking collectives: 14.2 us -> none  [local(): lax.all_to_all(frame_output[None], 'space', split_axis=1, concat_axis=2,...]
    ppermute x0 -> x3, waiting for transfers between devices: none -> 5.83 us  [local(): part = lax.ppermute(part, 'space', [(d, d ^ mask) for d in range(ways)])]
    ppermute x0 -> x3, starting transfers between devices: none -> 4.51 us  [local(): part = lax.ppermute(part, 'space', [(d, d ^ mask) for d in range(ways)])]
    dynamic_update_slice x0 -> x4, local copies, waits for them, and re-layouts: none -> 3.04 us  [local(): lax.dynamic_update_slice_in_dim(returned, part, (here ^ mask) * height, a...]
    unnamed x1 -> x0, other arithmetic: 2.21 us -> none
    another operation x1 -> x0, local copies, waits for them, and re-layouts: 1.35 us -> none  [local(): frame_output[None]]
    unnamed x11 -> x7, local copies, waits for them, and re-layouts: 6.28 us -> 5.4 us
  transfers between devices with their start and end apart: 5 -> 8, of which waited for: 2 -> 5; matrix products, arithmetic and copies ran while one was open for 6% -> 6% of each run, Pallas kernels for 0% -> 0%
where the time goes in v1:
time: 120 us; the launch traced here: 119 us
  local copies, waits for them, and re-layouts  32.7 us (27%)
  starting transfers between devices  20.3 us (17%)
  waiting for transfers between devices  15.8 us (13%)
  blocking collectives  15.5 us (13%)
  matrix products  12.8 us (11%)
  other arithmetic  11.1 us (9%)
  loops' own time  10.6 us (9%)
    all_gather x1, blocking collectives, local(): far_pair = lax.all_gather(pooled_heads[None], 'tm', axis=0, tiled=True)  15.5 us
    another operation x1, loops' own time, attend_frame(): results = lax.map(one_block, jnp.arange(block_count, dtype=jnp.int32))  10.6 us
    gather x4, local copies, waits for them, and re-layouts, one_block(): jnp.take(value_blocks, block_ids, axis=0)  7.12 us
    all_to_all x1, waiting for transfers between devices, local(): lax.all_to_all(values.reshape(split_shape), 'space', split_axis=2, concat...  6.76 us
    all_to_all x1, starting transfers between devices, local(): lax.all_to_all(key_tokens.reshape(split_shape), 'space', split_axis=2, co...  6.32 us
    ppermute x3, waiting for transfers between devices, local(): part = lax.ppermute(part, 'space', [(d, d ^ mask) for d in range(ways)])  5.83 us
    dot_general x4, matrix products, attend_block(): jnp.einsum('bhd,khd->hbk', query_rows, near_k, preferred_element_type=jnp...  5.48 us
    unnamed x7, local copies, waits for them, and re-layouts  5.4 us
  transfers between devices with their start and end apart: 8, of which 5 were waited for; matrix products, arithmetic and copies ran while one was open for 6% of the time, Pallas kernels for 0%

profile of v1, /device:TPU:0, one launch (start us, length us, event | category | flops | bytes accessed | tf_op | source)
XLA Modules:
  0.0 118.9 jit_solution(4346282646402476084)
XLA Ops:
  0.0 1.8 %copy.52 = bf16[1,256,512]{1,2,0:T(8,128)(2,1)} copy(bf16[1,256,512]{2,1,0:T(8,128)(2,1)} %param.12) | data formatting | bytes 524288 | tf_op args[1]
  1.8 6.3 %all-to-all-start = ((bf16[1,256,4,128]{1,3,0,2:T(8,128)(2,1)}), bf16[1,256,4,128]{1,3,0,2:T(8,128)(2,1)S(1)}, u32[]{:S(2)}, u32[]{:S(2)}) async-start(bf16[1,256,4,128]{1,3,0,2:T(8,128)(2,1)} %bitcast.2), calls=%async_computation | async-start | bytes 524288 | tf_op jit(solution)/shard_map/all_to_all | solution.py:132
  10.1 1.8 %copy.55 = bf16[1,256,512]{1,2,0:T(8,128)(2,1)} copy(bf16[1,256,512]{2,1,0:T(8,128)(2,1)} %param.13) | data formatting | bytes 524288 | tf_op args[2]
  11.9 1.8 %copy.58 = bf16[1,256,512]{1,2,0:T(8,128)(2,1)} copy(bf16[1,256,512]{2,1,0:T(8,128)(2,1)} %param.11) | data formatting | bytes 524288 | tf_op args[0]
  13.9 3.2 %all-to-all-done = bf16[1,256,4,128]{1,3,0,2:T(8,128)(2,1)S(1)} async-done(((bf16[1,256,4,128]{1,3,0,2:T(8,128)(2,1)}), bf16[1,256,4,128]{1,3,0,2:T(8,128)(2,1)S(1)}, u32[]{:S(2)}, u32[]{:S(2)}) %all-to-all-start) | async-done | bytes 262176 | tf_op jit(solution)/shard_map/all_to_all | solution.py:132
  17.0 3.4 %all-to-all-start.1 = ((bf16[1,256,4,128]{1,3,0,2:T(8,128)(2,1)}), bf16[1,256,4,128]{1,3,0,2:T(8,128)(2,1)S(1)}, u32[]{:S(2)}, u32[]{:S(2)}) async-start(bf16[1,256,4,128]{1,3,0,2:T(8,128)(2,1)} %bitcast.7), calls=%async_computation.1 | async-start | bytes 524288 | tf_op jit(solution)/shard_map/all_to_all | solution.py:135
  20.7 6.8 %all-to-all-done.1 = bf16[1,256,4,128]{1,3,0,2:T(8,128)(2,1)S(1)} async-done(((bf16[1,256,4,128]{1,3,0,2:T(8,128)(2,1)}), bf16[1,256,4,128]{1,3,0,2:T(8,128)(2,1)S(1)}, u32[]{:S(2)}, u32[]{:S(2)}) %all-to-all-start.1) | async-done | bytes 262176 | tf_op jit(solution)/shard_map/all_to_all | solution.py:135
  27.5 3.4 %all-to-all-start.2 = ((bf16[1,256,4,128]{1,3,0,2:T(8,128)(2,1)}), bf16[1,256,4,128]{1,3,0,2:T(8,128)(2,1)S(1)}, u32[]{:S(2)}, u32[]{:S(2)}) async-start(bf16[1,256,4,128]{1,3,0,2:T(8,128)(2,1)} %bitcast.13), calls=%async_computation.2 | async-start | bytes 524288 | tf_op jit(solution)/shard_map/all_to_all | solution.py:129
  31.1 1.3 %collective-permute-start = (bf16[1,2,1024,1,128]{4,2,3,1,0:T(8,128)(2,1)S(1)}, bf16[1,2,1024,1,128]{4,2,3,1,0:T(8,128)(2,1)S(1)}, u32[]{:S(2)}, u32[]{:S(2)}) collective-permute-start(bf16[1,2,1024,1,128]{4,2,3,1,0:T(8,128)(2,1)S(1)} %pad_maximum_fusion.1), channel_id=1, source_target_pairs={{0,4},{4,8},{8,12},{12,16},{16,20},{20,24},{24,28},{1,5},{5,9},{9,... | collective-permute-start | bytes 1572872 | tf_op jit(solution)/shard_map/ppermute | solution.py:17
  32.4 1.3 %collective-permute-start.1 = (bf16[1,2,1024,1,128]{4,2,3,1,0:T(8,128)(2,1)S(1)}, bf16[1,2,1024,1,128]{4,2,3,1,0:T(8,128)(2,1)S(1)}, u32[]{:S(2)}, u32[]{:S(2)}) collective-permute-start(bf16[1,2,1024,1,128]{4,2,3,1,0:T(8,128)(2,1)S(1)} %pad_maximum_fusion.1), channel_id=1, source_target_pairs={{4,0},{8,4},{12,8},{16,12},{20,16},{24,20},{28,24},{5,1},{9,5},{13... | collective-permute-start | bytes 1572872 | tf_op jit(solution)/shard_map/ppermute | solution.py:20
  33.8 15.5 %all-gather = bf16[16,8,128]{2,1,0:T(8,128)(2,1)S(1)} all-gather(bf16[2,8,128]{2,1,0:T(8,128)(2,1)S(1)} %multiply_convert_fusion.4), channel_id=2, replica_groups=mesh['tm'=8,'space'=4] {'tm'}, dimensions={0}, use_global_device_ids=true | all-gather | bytes 36864 | tf_op jit(solution)/shard_map/all_gather | solution.py:149
  51.7 51.8 %while.11 = (s32[]{:T(128)}, bf16[4,256,1,128]{3,1,0,2:T(8,128)(2,1)}, s32[4]{0:T(128)S(1)}, s32[4,8]{1,0:T(4,128)S(1)}, bf16[12,256,1,128]{3,1,0,2:T(8,128)(2,1...) while((s32[]{:T(128)}, ...), condition=%wide.region_12.14_spmd.clone, body=%wide.region_7.13_spmd.clone.sunk | while | flops 282329664 | bytes 14615961 | solution.py:118
  54.3 1.8 %gather_fusion = bf16[8,256,128]{2,1,0:T(8,128)(2,1)S(1)} fusion(bf16[12,256,128]{2,1,0:T(8,128)(2,1)} %bitcast.121, s32[1024]{0:T(1024)S(1)} %pad_clamp_fusion.2), kind=kCustom, calls=%fused_computation.clone.clone.1 | custom fusion | bytes 1048608 | tf_op jit(solution)/shard_map/while/body/eval_jaxpr/jit(_take)/gather | solution.py:111
  59.8 1.4 %fusion.57 = (f32[256]{0:T(256)S(1)}, f32[256,2048]{1,0:T(8,128)S(1)}) fusion(bf16[2048,128]{1,0:T(8,128)(2,1)S(1)} %bitcast.126, bf16[1024,1,128]{2,0,1:T(8,128)(2,1)} %get-tuple-element.271, s32[]{:T(128)S(6)} %select_n.192, pred[2048]{0:T(1024)(128)(4,1)S(1)} %broadcast_in_dim.262), kind=kOutput, calls=%fused_computation.79.clone.1 | convolution fusion | flops 135790336 | bytes 2690052 | tf_op jit(solution)/shard_map/while/body/eval_jaxpr/bhd,khd->hbk/dot_general | solution.py:51
  67.3 1.8 %gather_fusion = bf16[8,256,128]{2,1,0:T(8,128)(2,1)S(1)} fusion(bf16[12,256,128]{2,1,0:T(8,128)(2,1)} %bitcast.121, s32[1024]{0:T(1024)S(1)} %pad_clamp_fusion.2), kind=kCustom, calls=%fused_computation.clone.clone.1 | custom fusion | bytes 1048608 | tf_op jit(solution)/shard_map/while/body/eval_jaxpr/jit(_take)/gather | solution.py:111
  72.7 1.4 %fusion.57 = (f32[256]{0:T(256)S(1)}, f32[256,2048]{1,0:T(8,128)S(1)}) fusion(bf16[2048,128]{1,0:T(8,128)(2,1)S(1)} %bitcast.126, bf16[1024,1,128]{2,0,1:T(8,128)(2,1)} %get-tuple-element.271, s32[]{:T(128)S(6)} %select_n.192, pred[2048]{0:T(1024)(128)(4,1)S(1)} %broadcast_in_dim.262), kind=kOutput, calls=%fused_computation.79.clone.1 | convolution fusion | flops 135790336 | bytes 2690052 | tf_op jit(solution)/shard_map/while/body/eval_jaxpr/bhd,khd->hbk/dot_general | solution.py:51
  80.3 1.8 %gather_fusion = bf16[8,256,128]{2,1,0:T(8,128)(2,1)S(1)} fusion(bf16[12,256,128]{2,1,0:T(8,128)(2,1)} %bitcast.121, s32[1024]{0:T(1024)S(1)} %pad_clamp_fusion.2), kind=kCustom, calls=%fused_computation.clone.clone.1 | custom fusion | bytes 1048608 | tf_op jit(solution)/shard_map/while/body/eval_jaxpr/jit(_take)/gather | solution.py:111
  85.7 1.4 %fusion.57 = (f32[256]{0:T(256)S(1)}, f32[256,2048]{1,0:T(8,128)S(1)}) fusion(bf16[2048,128]{1,0:T(8,128)(2,1)S(1)} %bitcast.126, bf16[1024,1,128]{2,0,1:T(8,128)(2,1)} %get-tuple-element.271, s32[]{:T(128)S(6)} %select_n.192, pred[2048]{0:T(1024)(128)(4,1)S(1)} %broadcast_in_dim.262), kind=kOutput, calls=%fused_computation.79.clone.1 | convolution fusion | flops 135790336 | bytes 2690052 | tf_op jit(solution)/shard_map/while/body/eval_jaxpr/bhd,khd->hbk/dot_general | solution.py:51
  93.2 1.8 %gather_fusion = bf16[8,256,128]{2,1,0:T(8,128)(2,1)S(1)} fusion(bf16[12,256,128]{2,1,0:T(8,128)(2,1)} %bitcast.121, s32[1024]{0:T(1024)S(1)} %pad_clamp_fusion.2), kind=kCustom, calls=%fused_computation.clone.clone.1 | custom fusion | bytes 1048608 | tf_op jit(solution)/shard_map/while/body/eval_jaxpr/jit(_take)/gather | solution.py:111
  98.7 1.4 %fusion.57 = (f32[256]{0:T(256)S(1)}, f32[256,2048]{1,0:T(8,128)S(1)}) fusion(bf16[2048,128]{1,0:T(8,128)(2,1)S(1)} %bitcast.126, bf16[1024,1,128]{2,0,1:T(8,128)(2,1)} %get-tuple-element.271, s32[]{:T(128)S(6)} %select_n.192, pred[2048]{0:T(1024)(128)(4,1)S(1)} %broadcast_in_dim.262), kind=kOutput, calls=%fused_computation.79.clone.1 | convolution fusion | flops 135790336 | bytes 2690052 | tf_op jit(solution)/shard_map/while/body/eval_jaxpr/bhd,khd->hbk/dot_general | solution.py:51
  104.6 2.0 %collective-permute-start.2 = (bf16[1,256,1,128]{3,1,2,0:T(8,128)(2,1)S(1)}, bf16[1,256,1,128]{3,1,2,0:T(8,128)(2,1)S(1)}, u32[]{:S(2)}, u32[]{:S(2)}) collective-permute-start(bf16[1,256,1,128]{3,1,2,0:T(8,128)(2,1)S(1)} %get-tuple-element.134), channel_id=1, source_target_pairs={{0,1},{1,0},{2,3},{3,2},{4,5},{5,4},{6,7},{7,6},{8,9},{9,8},{10,11... | collective-permute-start | bytes 196616 | tf_op jit(solution)/shard_map/ppermute | solution.py:176
  106.6 2.4 %collective-permute-start.3 = (bf16[1,256,1,128]{3,1,2,0:T(8,128)(2,1)S(1)}, bf16[1,256,1,128]{3,1,2,0:T(8,128)(2,1)S(1)}, u32[]{:S(2)}, u32[]{:S(2)}) collective-permute-start(bf16[1,256,1,128]{3,1,2,0:T(8,128)(2,1)S(1)} %get-tuple-element.133), channel_id=1, source_target_pairs={{0,2},{1,3},{2,0},{3,1},{4,6},{5,7},{6,4},{7,5},{8,10},{9,11},{10,... | collective-permute-start | bytes 196616 | tf_op jit(solution)/shard_map/ppermute | solution.py:176
  109.2 5.0 %collective-permute-done.3 = bf16[1,256,1,128]{3,1,2,0:T(8,128)(2,1)S(1)} collective-permute-done((bf16[1,256,1,128]{3,1,2,0:T(8,128)(2,1)S(1)}, bf16[1,256,1,128]{3,1,2,0:T(8,128)(2,1)S(1)}, u32[]{:S(2)}, u32[]{:S(2)}) %collective-permute-start.3) | collective-permute-done | bytes 65568 | tf_op jit(solution)/shard_map/ppermute | solution.py:176
  115.3 2.8 %dynamic_update_slice.19 = bf16[1,256,4,128]{3,2,1,0:T(4,128)(2,1)S(1)} dynamic-update-slice(bf16[1,256,4,128]{3,2,1,0:T(4,128)(2,1)S(1)} %copy.62, bf16[1,256,1,128]{3,2,1,0:T(2,128)(2,1)S(1)} %copy.63, s32[]{:T(128)} %constant.46.clone.1, s32[]{:T(128)} %constant.46.clone.1, s32[]{:T(128)S(6)} %select_n.143, s32[]{:T(128)} %constant.46.clone.1) | dynamic-update-slice | bytes 131076 | tf_op jit(solution)/shard_map/dynamic_update_slice | solution.py:177
  (150 shorter events, 36.6 us)
Async XLA Ops:
  0.0 20.5 %copy-start = (s32[8,4,8]{2,1,0:T(4,128)S(1)}, s32[8,4,8]{2,1,0:T(4,128)}, u32[]{:S(2)}) copy-start(s32[8,4,8]{2,1,0:T(4,128)} %param.14) | copy-start | bytes 3076
  0.0 13.7 %copy-start.2 = (s32[8,4]{0,1:T(4,128)S(1)}, s32[8,4]{0,1:T(4,128)}, u32[]{:S(2)}) copy-start(s32[8,4]{0,1:T(4,128)} %param.15) | copy-start | bytes 388
  1.8 15.2 %all-to-all-start = ((bf16[1,256,4,128]{1,3,0,2:T(8,128)(2,1)}), bf16[1,256,4,128]{1,3,0,2:T(8,128)(2,1)S(1)}, u32[]{:S(2)}, u32[]{:S(2)}) async-start(bf16[1,256,4,128]{1,3,0,2:T(8,128)(2,1)} %bitcast.2), calls=%async_computation | async-start | bytes 524288 | tf_op jit(solution)/shard_map/all_to_all | solution.py:132
  17.0 10.4 %all-to-all-start.1 = ((bf16[1,256,4,128]{1,3,0,2:T(8,128)(2,1)}), bf16[1,256,4,128]{1,3,0,2:T(8,128)(2,1)S(1)}, u32[]{:S(2)}, u32[]{:S(2)}) async-start(bf16[1,256,4,128]{1,3,0,2:T(8,128)(2,1)} %bitcast.7), calls=%async_computation.1 | async-start | bytes 524288 | tf_op jit(solution)/shard_map/all_to_all | solution.py:135
  27.5 22.1 %all-to-all-start.2 = ((bf16[1,256,4,128]{1,3,0,2:T(8,128)(2,1)}), bf16[1,256,4,128]{1,3,0,2:T(8,128)(2,1)S(1)}, u32[]{:S(2)}, u32[]{:S(2)}) async-start(bf16[1,256,4,128]{1,3,0,2:T(8,128)(2,1)} %bitcast.13), calls=%async_computation.2 | async-start | bytes 524288 | tf_op jit(solution)/shard_map/all_to_all | solution.py:129
  31.1 19.4 %collective-permute-start = (bf16[1,2,1024,1,128]{4,2,3,1,0:T(8,128)(2,1)S(1)}, bf16[1,2,1024,1,128]{4,2,3,1,0:T(8,128)(2,1)S(1)}, u32[]{:S(2)}, u32[]{:S(2)}) collective-permute-start(bf16[1,2,1024,1,128]{4,2,3,1,0:T(8,128)(2,1)S(1)} %pad_maximum_fusion.1), channel_id=1, source_target_pairs={{0,4},{4,8},{8,12},{12,16},{16,20},{20,24},{24,28},{1,5},{5,9},{9,... | collective-permute-start | bytes 1572872 | tf_op jit(solution)/shard_map/ppermute | solution.py:17
  32.4 18.1 %collective-permute-start.1 = (bf16[1,2,1024,1,128]{4,2,3,1,0:T(8,128)(2,1)S(1)}, bf16[1,2,1024,1,128]{4,2,3,1,0:T(8,128)(2,1)S(1)}, u32[]{:S(2)}, u32[]{:S(2)}) collective-permute-start(bf16[1,2,1024,1,128]{4,2,3,1,0:T(8,128)(2,1)S(1)} %pad_maximum_fusion.1), channel_id=1, source_target_pairs={{4,0},{8,4},{12,8},{16,12},{20,16},{24,20},{28,24},{5,1},{9,5},{13... | collective-permute-start | bytes 1572872 | tf_op jit(solution)/shard_map/ppermute | solution.py:20
  61.2 2.2 %copy-start.1 = (bf16[8,256,1,128]{3,1,0,2:T(8,128)(2,1)S(1)}, bf16[8,256,1,128]{3,1,0,2:T(8,128)(2,1)}, u32[]{:S(2)}) copy-start(bf16[8,256,1,128]{3,1,0,2:T(8,128)(2,1)} %get-tuple-element.229) | copy-start | bytes 1572868 | tf_op jit(solution)/shard_map/while
  74.1 2.2 %copy-start.1 = (bf16[8,256,1,128]{3,1,0,2:T(8,128)(2,1)S(1)}, bf16[8,256,1,128]{3,1,0,2:T(8,128)(2,1)}, u32[]{:S(2)}) copy-start(bf16[8,256,1,128]{3,1,0,2:T(8,128)(2,1)} %get-tuple-element.229) | copy-start | bytes 1572868 | tf_op jit(solution)/shard_map/while
  87.1 2.2 %copy-start.1 = (bf16[8,256,1,128]{3,1,0,2:T(8,128)(2,1)S(1)}, bf16[8,256,1,128]{3,1,0,2:T(8,128)(2,1)}, u32[]{:S(2)}) copy-start(bf16[8,256,1,128]{3,1,0,2:T(8,128)(2,1)} %get-tuple-element.229) | copy-start | bytes 1572868 | tf_op jit(solution)/shard_map/while
  100.0 2.2 %copy-start.1 = (bf16[8,256,1,128]{3,1,0,2:T(8,128)(2,1)S(1)}, bf16[8,256,1,128]{3,1,0,2:T(8,128)(2,1)}, u32[]{:S(2)}) copy-start(bf16[8,256,1,128]{3,1,0,2:T(8,128)(2,1)} %get-tuple-element.229) | copy-start | bytes 1572868 | tf_op jit(solution)/shard_map/while
  104.6 4.6 %collective-permute-start.2 = (bf16[1,256,1,128]{3,1,2,0:T(8,128)(2,1)S(1)}, bf16[1,256,1,128]{3,1,2,0:T(8,128)(2,1)S(1)}, u32[]{:S(2)}, u32[]{:S(2)}) collective-permute-start(bf16[1,256,1,128]{3,1,2,0:T(8,128)(2,1)S(1)} %get-tuple-element.134), channel_id=1, source_target_pairs={{0,1},{1,0},{2,3},{3,2},{4,5},{5,4},{6,7},{7,6},{8,9},{9,8},{10,11... | collective-permute-start | bytes 196616 | tf_op jit(solution)/shard_map/ppermute | solution.py:176
  106.6 7.6 %collective-permute-start.3 = (bf16[1,256,1,128]{3,1,2,0:T(8,128)(2,1)S(1)}, bf16[1,256,1,128]{3,1,2,0:T(8,128)(2,1)S(1)}, u32[]{:S(2)}, u32[]{:S(2)}) collective-permute-start(bf16[1,256,1,128]{3,1,2,0:T(8,128)(2,1)S(1)} %get-tuple-element.133), channel_id=1, source_target_pairs={{0,2},{1,3},{2,0},{3,1},{4,6},{5,7},{6,4},{7,5},{8,10},{9,11},{10,... | collective-permute-start | bytes 196616 | tf_op jit(solution)/shard_map/ppermute | solution.py:176
  109.0 6.2 %collective-permute-start.4 = (bf16[1,256,1,128]{3,1,2,0:T(8,128)(2,1)S(1)}, bf16[1,256,1,128]{3,1,2,0:T(8,128)(2,1)S(1)}, u32[]{:S(2)}, u32[]{:S(2)}) collective-permute-start(bf16[1,256,1,128]{3,1,2,0:T(8,128)(2,1)S(1)} %get-tuple-element.132), channel_id=1, source_target_pairs={{0,3},{1,2},{2,1},{3,0},{4,7},{5,6},{6,5},{7,4},{8,11},{9,10},{10,... | collective-permute-start | bytes 196616 | tf_op jit(solution)/shard_map/ppermute | solution.py:176
